TPU v7x, 32 devices: a whole 2x2x4 slice. The times are simulated.
32 devices in a mesh: group: 2 (over y), snp: 4 (over x, core), ind: 4 (over z).
Axes of the slice: x: 2, y: 2, z: 4, core: 2. Of those that a mesh axis runs over, the one named last changes fastest.
Arguments:
- genotypes: int32 [8192, 8192], P(('group', 'ind'), 'snp'), parts along dimension 0, may hold values from 0 to 255, as said below
- ancestry: float32 [64, 32768], P(None, ('group', 'ind')), parts along dimension 1, may hold values from 0 to 1, as said below
- frequency: float32 [64, 16384], P(None, ('group', 'snp')), parts along dimension 1, may hold values from 0.05 to 0.95
Outputs:
- ancestry_new: float32 [64, 32768], P(None, ('group', 'ind')), parts along dimension 1
- frequency_new: float32 [64, 16384], P(None, ('group', 'snp')), parts along dimension 1
There are 2 independent parts, one for each index of `group`. A program takes and returns all parts, laid end to end along the dimension named above; each array names one. Nothing has to cross between parts.
Inputs may be any that keep to these rules, and one draw needn't show every extreme that they name: `genotypes`: each word holds four 2-bit codes as in the first step; every code is 0, 1, 2 (allele count) or 3 (missing). `ancestry`: entries are positive and each individual's column sums to one.
All inputs are finite; a program needn't handle non-finite values.
Results may differ from a plain program's by a relative error of at most 0.0003.
Values sent between devices are 32-bit elements; how exact they have to be, the bound alone decides.
A program may use at most 64 MiB of HBM per device.

v0:
```python
import jax
import jax.numpy as jnp
from jax import lax
from jax.sharding import PartitionSpec as P

SNP_BLOCK = 256


def unpack(words):
    shifts = 2 * jnp.arange(4, dtype=jnp.int32)
    codes = words[None] >> shifts[:, None, None] & 3
    return codes.reshape(4 * words.shape[0], words.shape[1])


def over_rows(left, right):
    return lax.dot_general(
        left, right, (((0,), (0,)), ((), ())), preferred_element_type=jnp.float32
    )


def over_columns(left, right):
    return lax.dot_general(
        left, right, (((1,), (1,)), ((), ())), preferred_element_type=jnp.float32
    )


def block_terms(words, q_half, f_block, rest_block):
    codes = unpack(words)
    mixed = over_rows(q_half, f_block)
    seen = codes < 3
    counts = codes.astype(jnp.float32)
    ratio_a = jnp.where(seen, counts / mixed, 0.0).astype(jnp.bfloat16)
    ratio_b = jnp.where(seen, (2.0 - counts) / (1.0 - mixed), 0.0).astype(jnp.bfloat16)
    stat = over_columns(f_block, ratio_a) + over_columns(rest_block, ratio_b)
    allele_a = jnp.dot(q_half, ratio_a, preferred_element_type=jnp.float32)
    allele_b = jnp.dot(q_half, ratio_b, preferred_element_type=jnp.float32)
    return (stat, allele_a, allele_b)


def rescale(weights, stat, populations):
    weighted = weights * stat
    return populations * weighted / jnp.sum(weighted, axis=0, keepdims=True)


def refresh(current, allele_a, allele_b):
    upper_part = current * allele_a
    return upper_part / (upper_part + (1.0 - current) * allele_b)


def on_device(genotypes, ancestry, frequency):
    populations = ancestry.shape[0]
    people = ancestry.shape[1]
    columns = frequency.shape[1]
    blocks = columns // SNP_BLOCK
    q_half = ancestry.astype(jnp.bfloat16)
    f_half = frequency.astype(jnp.bfloat16)
    rest_half = (1.0 - frequency).astype(jnp.bfloat16)
    empty_stat = jnp.zeros((populations, people), jnp.float32)

    def terms(start):
        words = lax.dynamic_slice_in_dim(genotypes, start, SNP_BLOCK, 1)
        f_block = lax.dynamic_slice_in_dim(f_half, start, SNP_BLOCK, 1)
        rest_block = lax.dynamic_slice_in_dim(rest_half, start, SNP_BLOCK, 1)
        return block_terms(words, q_half, f_block, rest_block)

    def sweep_after(index, carry):
        stat_total, totals_a, totals_b = carry
        start = index * SNP_BLOCK
        stat, allele_a, allele_b = terms(start)
        totals_a = lax.dynamic_update_slice_in_dim(totals_a, allele_a, start, 1)
        totals_b = lax.dynamic_update_slice_in_dim(totals_b, allele_b, start, 1)
        return (stat_total + stat, totals_a, totals_b)

    empty_cols = jnp.zeros_like(frequency)
    stat_total, totals_a, totals_b = lax.fori_loop(
        0, blocks, sweep_after, (empty_stat, empty_cols, empty_cols)
    )
    totals_a, totals_b = lax.psum((totals_a, totals_b), "ind")
    frequency_new = refresh(frequency, totals_a, totals_b)
    share = lax.psum_scatter(stat_total, "snp", scatter_dimension=1, tiled=True)
    span_ind = share.shape[1]
    owned = lax.dynamic_slice_in_dim(ancestry, lax.axis_index("snp") * span_ind, span_ind, 1)
    ancestry_new = lax.all_gather(rescale(owned, share, populations), "snp", axis=1, tiled=True)
    return (ancestry_new, frequency_new)


def solution(mesh):
    placed = (P(("group", "ind"), "snp"), P(None, ("group", "ind")), P(None, ("group", "snp")))
    return jax.shard_map(
        on_device,
        mesh=mesh,
        in_specs=placed,
        out_specs=(P(None, ("group", "ind")), P(None, ("group", "snp"))),
        check_vma=False,
    )
```

profile of v0, /device:TPU:0, one launch (start us, length us, event | category | flops | bytes accessed | tf_op | source)
XLA Modules:
  0.0 238.7 jit_solution(4005182025819725949)
XLA Ops:
  12.3 156.0 %while.18 = (s32[]{:T(128)}, f32[64,4096]{1,0:T(8,128)}, f32[64,2048]{1,0:T(8,128)}, f32[64,2048]{1,0:T(8,128)}, bf16[64,2048]{1,0:T(8,128)(2,1)S(1)}, /*index=5...) while((s32[]{:T(128)}, f32[64,4096]{1,0:T(8,128)}, ...), condition=%wide.region_1.2_spmd.clone, body=%wide.region_0.1_spmd.clone.sunk | while | flops 684457984 | bytes 63734156 | solution.py:75
  15.4 3.8 %copy.15 = s32[32,8,4,1024]{3,1,2,0:T(8,128)S(1)} copy(s32[32,8,4,1024]{3,2,1,0:T(4,128)S(1)} %bitcast.52) | data formatting | bytes 8388608 | tf_op jit(solution)/shard_map/while
  19.3 2.2 select_convert_fusion.3
  25.9 2.4 %fusion.43 = f32[64,2048]{1,0:T(8,128)} fusion(f32[64,2048]{1,0:T(8,128)} %get-tuple-element.270, s32[]{:T(128)S(6)} %select_n.38, bf16[4096,256]{0,1:T(8,128)(2,1)S(1)} %copy-done.1, bf16[64,4096]{1,0:T(8,128)(2,1)} %copy-done.2), kind=kOutput, calls=%fused_computation.10.clone.1 | convolution fusion | flops 134217728 | bytes 2686980 | tf_op jit(solution)/shard_map/while/body/eval_jaxpr/dot_general | solution.py:35
  28.4 2.4 %fusion.44 = f32[64,2048]{1,0:T(8,128)} fusion(f32[64,2048]{1,0:T(8,128)} %get-tuple-element.271, s32[]{:T(128)S(6)} %select_n.38, bf16[4096,256]{0,1:T(8,128)(2,1)S(1)} %get-tuple-element.255, bf16[64,4096]{1,0:T(8,128)(2,1)} %copy-done.2), kind=kOutput, calls=%fused_computation.8.clone.1 | convolution fusion | flops 134217728 | bytes 2686980 | tf_op jit(solution)/shard_map/while/body/eval_jaxpr/dot_general | solution.py:36
  30.8 1.6 constant_dynamic-slice_fusion.2
  33.9 3.8 %copy.15 = s32[32,8,4,1024]{3,1,2,0:T(8,128)S(1)} copy(s32[32,8,4,1024]{3,2,1,0:T(4,128)S(1)} %bitcast.52) | data formatting | bytes 8388608 | tf_op jit(solution)/shard_map/while
  37.8 2.2 select_convert_fusion.3
  42.6 2.8 %fusion.42 = f32[64,4096]{1,0:T(8,128)} fusion(f32[64,4096]{1,0:T(8,128)S(1)} %fusion.41, bf16[4096,256]{0,1:T(8,128)(2,1)S(1)} %get-tuple-element.255, f32[64,4096]{1,0:T(8,128)} %get-tuple-element.269, pred[]{:T(512)S(6)} %compare.3, bf16[64,2048]{1,0:T(8,128)(2,1)S(1)} %get-tuple-element.287, s32[]{:T(128)S(6)} %select_n.38), kind=kOutput, calls=%fused_computation.2.clone.1 | convolution fusion | flops 135004160 | bytes 5275653 | tf_op jit(solution)/shard_map/while/body/eval_jaxpr/dot_general | solution.py:22
  45.5 2.5 %fusion.43 = f32[64,2048]{1,0:T(8,128)} fusion(f32[64,2048]{1,0:T(8,128)} %get-tuple-element.270, s32[]{:T(128)S(6)} %select_n.38, bf16[4096,256]{0,1:T(8,128)(2,1)S(1)} %copy-done.1, bf16[64,4096]{1,0:T(8,128)(2,1)} %copy-done.2), kind=kOutput, calls=%fused_computation.10.clone.1 | convolution fusion | flops 134217728 | bytes 2686980 | tf_op jit(solution)/shard_map/while/body/eval_jaxpr/dot_general | solution.py:35
  48.0 2.4 %fusion.44 = f32[64,2048]{1,0:T(8,128)} fusion(f32[64,2048]{1,0:T(8,128)} %get-tuple-element.271, s32[]{:T(128)S(6)} %select_n.38, bf16[4096,256]{0,1:T(8,128)(2,1)S(1)} %get-tuple-element.255, bf16[64,4096]{1,0:T(8,128)(2,1)} %copy-done.2), kind=kOutput, calls=%fused_computation.8.clone.1 | convolution fusion | flops 134217728 | bytes 2686980 | tf_op jit(solution)/shard_map/while/body/eval_jaxpr/dot_general | solution.py:36
  50.5 1.6 constant_dynamic-slice_fusion.2
  53.6 3.8 %copy.15 = s32[32,8,4,1024]{3,1,2,0:T(8,128)S(1)} copy(s32[32,8,4,1024]{3,2,1,0:T(4,128)S(1)} %bitcast.52) | data formatting | bytes 8388608 | tf_op jit(solution)/shard_map/while
  57.5 2.2 select_convert_fusion.3
  62.3 2.8 %fusion.42 = f32[64,4096]{1,0:T(8,128)} fusion(f32[64,4096]{1,0:T(8,128)S(1)} %fusion.41, bf16[4096,256]{0,1:T(8,128)(2,1)S(1)} %get-tuple-element.255, f32[64,4096]{1,0:T(8,128)} %get-tuple-element.269, pred[]{:T(512)S(6)} %compare.3, bf16[64,2048]{1,0:T(8,128)(2,1)S(1)} %get-tuple-element.287, s32[]{:T(128)S(6)} %select_n.38), kind=kOutput, calls=%fused_computation.2.clone.1 | convolution fusion | flops 135004160 | bytes 5275653 | tf_op jit(solution)/shard_map/while/body/eval_jaxpr/dot_general | solution.py:22
  65.1 2.5 %fusion.43 = f32[64,2048]{1,0:T(8,128)} fusion(f32[64,2048]{1,0:T(8,128)} %get-tuple-element.270, s32[]{:T(128)S(6)} %select_n.38, bf16[4096,256]{0,1:T(8,128)(2,1)S(1)} %copy-done.1, bf16[64,4096]{1,0:T(8,128)(2,1)} %copy-done.2), kind=kOutput, calls=%fused_computation.10.clone.1 | convolution fusion | flops 134217728 | bytes 2686980 | tf_op jit(solution)/shard_map/while/body/eval_jaxpr/dot_general | solution.py:35
  67.6 2.4 %fusion.44 = f32[64,2048]{1,0:T(8,128)} fusion(f32[64,2048]{1,0:T(8,128)} %get-tuple-element.271, s32[]{:T(128)S(6)} %select_n.38, bf16[4096,256]{0,1:T(8,128)(2,1)S(1)} %get-tuple-element.255, bf16[64,4096]{1,0:T(8,128)(2,1)} %copy-done.2), kind=kOutput, calls=%fused_computation.8.clone.1 | convolution fusion | flops 134217728 | bytes 2686980 | tf_op jit(solution)/shard_map/while/body/eval_jaxpr/dot_general | solution.py:36
  70.1 1.6 constant_dynamic-slice_fusion.2
  73.2 3.8 %copy.15 = s32[32,8,4,1024]{3,1,2,0:T(8,128)S(1)} copy(s32[32,8,4,1024]{3,2,1,0:T(4,128)S(1)} %bitcast.52) | data formatting | bytes 8388608 | tf_op jit(solution)/shard_map/while
  77.1 2.2 select_convert_fusion.3
  81.9 2.8 %fusion.42 = f32[64,4096]{1,0:T(8,128)} fusion(f32[64,4096]{1,0:T(8,128)S(1)} %fusion.41, bf16[4096,256]{0,1:T(8,128)(2,1)S(1)} %get-tuple-element.255, f32[64,4096]{1,0:T(8,128)} %get-tuple-element.269, pred[]{:T(512)S(6)} %compare.3, bf16[64,2048]{1,0:T(8,128)(2,1)S(1)} %get-tuple-element.287, s32[]{:T(128)S(6)} %select_n.38), kind=kOutput, calls=%fused_computation.2.clone.1 | convolution fusion | flops 135004160 | bytes 5275653 | tf_op jit(solution)/shard_map/while/body/eval_jaxpr/dot_general | solution.py:22
  84.8 2.5 %fusion.43 = f32[64,2048]{1,0:T(8,128)} fusion(f32[64,2048]{1,0:T(8,128)} %get-tuple-element.270, s32[]{:T(128)S(6)} %select_n.38, bf16[4096,256]{0,1:T(8,128)(2,1)S(1)} %copy-done.1, bf16[64,4096]{1,0:T(8,128)(2,1)} %copy-done.2), kind=kOutput, calls=%fused_computation.10.clone.1 | convolution fusion | flops 134217728 | bytes 2686980 | tf_op jit(solution)/shard_map/while/body/eval_jaxpr/dot_general | solution.py:35
  87.3 2.5 %fusion.44 = f32[64,2048]{1,0:T(8,128)} fusion(f32[64,2048]{1,0:T(8,128)} %get-tuple-element.271, s32[]{:T(128)S(6)} %select_n.38, bf16[4096,256]{0,1:T(8,128)(2,1)S(1)} %get-tuple-element.255, bf16[64,4096]{1,0:T(8,128)(2,1)} %copy-done.2), kind=kOutput, calls=%fused_computation.8.clone.1 | convolution fusion | flops 134217728 | bytes 2686980 | tf_op jit(solution)/shard_map/while/body/eval_jaxpr/dot_general | solution.py:36
  92.9 3.8 %copy.15 = s32[32,8,4,1024]{3,1,2,0:T(8,128)S(1)} copy(s32[32,8,4,1024]{3,2,1,0:T(4,128)S(1)} %bitcast.52) | data formatting | bytes 8388608 | tf_op jit(solution)/shard_map/while
  96.8 2.2 select_convert_fusion.3
  101.6 2.8 %fusion.42 = f32[64,4096]{1,0:T(8,128)} fusion(f32[64,4096]{1,0:T(8,128)S(1)} %fusion.41, bf16[4096,256]{0,1:T(8,128)(2,1)S(1)} %get-tuple-element.255, f32[64,4096]{1,0:T(8,128)} %get-tuple-element.269, pred[]{:T(512)S(6)} %compare.3, bf16[64,2048]{1,0:T(8,128)(2,1)S(1)} %get-tuple-element.287, s32[]{:T(128)S(6)} %select_n.38), kind=kOutput, calls=%fused_computation.2.clone.1 | convolution fusion | flops 135004160 | bytes 5275653 | tf_op jit(solution)/shard_map/while/body/eval_jaxpr/dot_general | solution.py:22
  104.5 2.5 %fusion.43 = f32[64,2048]{1,0:T(8,128)} fusion(f32[64,2048]{1,0:T(8,128)} %get-tuple-element.270, s32[]{:T(128)S(6)} %select_n.38, bf16[4096,256]{0,1:T(8,128)(2,1)S(1)} %copy-done.1, bf16[64,4096]{1,0:T(8,128)(2,1)} %copy-done.2), kind=kOutput, calls=%fused_computation.10.clone.1 | convolution fusion | flops 134217728 | bytes 2686980 | tf_op jit(solution)/shard_map/while/body/eval_jaxpr/dot_general | solution.py:35
  107.0 2.4 %fusion.44 = f32[64,2048]{1,0:T(8,128)} fusion(f32[64,2048]{1,0:T(8,128)} %get-tuple-element.271, s32[]{:T(128)S(6)} %select_n.38, bf16[4096,256]{0,1:T(8,128)(2,1)S(1)} %get-tuple-element.255, bf16[64,4096]{1,0:T(8,128)(2,1)} %copy-done.2), kind=kOutput, calls=%fused_computation.8.clone.1 | convolution fusion | flops 134217728 | bytes 2686980 | tf_op jit(solution)/shard_map/while/body/eval_jaxpr/dot_general | solution.py:36
  112.5 3.8 %copy.15 = s32[32,8,4,1024]{3,1,2,0:T(8,128)S(1)} copy(s32[32,8,4,1024]{3,2,1,0:T(4,128)S(1)} %bitcast.52) | data formatting | bytes 8388608 | tf_op jit(solution)/shard_map/while
  116.4 2.2 select_convert_fusion.3
  121.2 2.8 %fusion.42 = f32[64,4096]{1,0:T(8,128)} fusion(f32[64,4096]{1,0:T(8,128)S(1)} %fusion.41, bf16[4096,256]{0,1:T(8,128)(2,1)S(1)} %get-tuple-element.255, f32[64,4096]{1,0:T(8,128)} %get-tuple-element.269, pred[]{:T(512)S(6)} %compare.3, bf16[64,2048]{1,0:T(8,128)(2,1)S(1)} %get-tuple-element.287, s32[]{:T(128)S(6)} %select_n.38), kind=kOutput, calls=%fused_computation.2.clone.1 | convolution fusion | flops 135004160 | bytes 5275653 | tf_op jit(solution)/shard_map/while/body/eval_jaxpr/dot_general | solution.py:22
  124.1 2.5 %fusion.43 = f32[64,2048]{1,0:T(8,128)} fusion(f32[64,2048]{1,0:T(8,128)} %get-tuple-element.270, s32[]{:T(128)S(6)} %select_n.38, bf16[4096,256]{0,1:T(8,128)(2,1)S(1)} %copy-done.1, bf16[64,4096]{1,0:T(8,128)(2,1)} %copy-done.2), kind=kOutput, calls=%fused_computation.10.clone.1 | convolution fusion | flops 134217728 | bytes 2686980 | tf_op jit(solution)/shard_map/while/body/eval_jaxpr/dot_general | solution.py:35
  126.6 2.4 %fusion.44 = f32[64,2048]{1,0:T(8,128)} fusion(f32[64,2048]{1,0:T(8,128)} %get-tuple-element.271, s32[]{:T(128)S(6)} %select_n.38, bf16[4096,256]{0,1:T(8,128)(2,1)S(1)} %get-tuple-element.255, bf16[64,4096]{1,0:T(8,128)(2,1)} %copy-done.2), kind=kOutput, calls=%fused_computation.8.clone.1 | convolution fusion | flops 134217728 | bytes 2686980 | tf_op jit(solution)/shard_map/while/body/eval_jaxpr/dot_general | solution.py:36
  132.2 3.8 %copy.15 = s32[32,8,4,1024]{3,1,2,0:T(8,128)S(1)} copy(s32[32,8,4,1024]{3,2,1,0:T(4,128)S(1)} %bitcast.52) | data formatting | bytes 8388608 | tf_op jit(solution)/shard_map/while
  136.1 2.2 select_convert_fusion.3
  140.9 2.8 %fusion.42 = f32[64,4096]{1,0:T(8,128)} fusion(f32[64,4096]{1,0:T(8,128)S(1)} %fusion.41, bf16[4096,256]{0,1:T(8,128)(2,1)S(1)} %get-tuple-element.255, f32[64,4096]{1,0:T(8,128)} %get-tuple-element.269, pred[]{:T(512)S(6)} %compare.3, bf16[64,2048]{1,0:T(8,128)(2,1)S(1)} %get-tuple-element.287, s32[]{:T(128)S(6)} %select_n.38), kind=kOutput, calls=%fused_computation.2.clone.1 | convolution fusion | flops 135004160 | bytes 5275653 | tf_op jit(solution)/shard_map/while/body/eval_jaxpr/dot_general | solution.py:22
  143.7 2.5 %fusion.43 = f32[64,2048]{1,0:T(8,128)} fusion(f32[64,2048]{1,0:T(8,128)} %get-tuple-element.270, s32[]{:T(128)S(6)} %select_n.38, bf16[4096,256]{0,1:T(8,128)(2,1)S(1)} %copy-done.1, bf16[64,4096]{1,0:T(8,128)(2,1)} %copy-done.2), kind=kOutput, calls=%fused_computation.10.clone.1 | convolution fusion | flops 134217728 | bytes 2686980 | tf_op jit(solution)/shard_map/while/body/eval_jaxpr/dot_general | solution.py:35
  146.2 2.4 %fusion.44 = f32[64,2048]{1,0:T(8,128)} fusion(f32[64,2048]{1,0:T(8,128)} %get-tuple-element.271, s32[]{:T(128)S(6)} %select_n.38, bf16[4096,256]{0,1:T(8,128)(2,1)S(1)} %get-tuple-element.255, bf16[64,4096]{1,0:T(8,128)(2,1)} %copy-done.2), kind=kOutput, calls=%fused_computation.8.clone.1 | convolution fusion | flops 134217728 | bytes 2686980 | tf_op jit(solution)/shard_map/while/body/eval_jaxpr/dot_general | solution.py:36
  151.8 3.8 %copy.15 = s32[32,8,4,1024]{3,1,2,0:T(8,128)S(1)} copy(s32[32,8,4,1024]{3,2,1,0:T(4,128)S(1)} %bitcast.52) | data formatting | bytes 8388608 | tf_op jit(solution)/shard_map/while
  155.7 2.2 select_convert_fusion.3
  160.5 2.8 %fusion.42 = f32[64,4096]{1,0:T(8,128)} fusion(f32[64,4096]{1,0:T(8,128)S(1)} %fusion.41, bf16[4096,256]{0,1:T(8,128)(2,1)S(1)} %get-tuple-element.255, f32[64,4096]{1,0:T(8,128)} %get-tuple-element.269, pred[]{:T(512)S(6)} %compare.3, bf16[64,2048]{1,0:T(8,128)(2,1)S(1)} %get-tuple-element.287, s32[]{:T(128)S(6)} %select_n.38), kind=kOutput, calls=%fused_computation.2.clone.1 | convolution fusion | flops 135004160 | bytes 5275653 | tf_op jit(solution)/shard_map/while/body/eval_jaxpr/dot_general | solution.py:22
  163.4 2.5 %fusion.43 = f32[64,2048]{1,0:T(8,128)} fusion(f32[64,2048]{1,0:T(8,128)} %get-tuple-element.270, s32[]{:T(128)S(6)} %select_n.38, bf16[4096,256]{0,1:T(8,128)(2,1)S(1)} %copy-done.1, bf16[64,4096]{1,0:T(8,128)(2,1)} %copy-done.2), kind=kOutput, calls=%fused_computation.10.clone.1 | convolution fusion | flops 134217728 | bytes 2686980 | tf_op jit(solution)/shard_map/while/body/eval_jaxpr/dot_general | solution.py:35
  165.9 2.4 %fusion.44 = f32[64,2048]{1,0:T(8,128)} fusion(f32[64,2048]{1,0:T(8,128)} %get-tuple-element.271, s32[]{:T(128)S(6)} %select_n.38, bf16[4096,256]{0,1:T(8,128)(2,1)S(1)} %get-tuple-element.255, bf16[64,4096]{1,0:T(8,128)(2,1)} %copy-done.2), kind=kOutput, calls=%fused_computation.8.clone.1 | convolution fusion | flops 134217728 | bytes 2686980 | tf_op jit(solution)/shard_map/while/body/eval_jaxpr/dot_general | solution.py:36
  169.0 27.2 %reduce-scatter.2.cloned.1.call-done = f32[64,1024]{1,0:T(8,128)} async-done(((f32[64,4096]{1,0:T(8,128)}), f32[64,1024]{1,0:T(8,128)}) %reduce-scatter.2.cloned.1.call-update) | async-done | bytes 262160 | tf_op jit(solution)/shard_map/reduce_scatter | solution.py:80
  197.2 1.8 multiply_divide_fusion
  199.0 27.7 %all-reduce.3.cloned.1.call-done = (f32[64,2048]{1,0:T(8,128)}, f32[64,2048]{1,0:T(8,128)}) async-done(((f32[64,2048]{1,0:T(8,128)}, f32[64,2048]{1,0:T(8,128)}), (f32[64,2048]{1,0:T(8,128)}, f32[64,2048]{1,0:T(8,128)})) %all-reduce.3.cloned.1.call-update) | async-done | bytes 1048592 | tf_op jit(solution)/shard_map/psum | solution.py:78
  226.8 2.3 add_divide_fusion
  229.0 2.3 copy.34
  (163 shorter events, 49.2 us)
Async XLA Ops:
  8.0 188.2 %reduce-scatter.2.cloned.1.call-start = ((), (), s32[]{:S(2)}) async-start(), calls=%async_computation.1 | async-start | bytes 1310720 | tf_op jit(solution)/shard_map/reduce_scatter | solution.py:80
  12.3 7.0 %copy-start.2 = (bf16[64,4096]{1,0:T(8,128)(2,1)}, bf16[64,4096]{1,0:T(8,128)(2,1)S(1)}, u32[]{:S(2)}) copy-start(bf16[64,4096]{1,0:T(8,128)(2,1)S(1)} %get-tuple-element.286) | copy-start | bytes 1572868 | tf_op jit(solution)/shard_map/while
  12.3 7.0 %copy-start.4 = (bf16[64,2048]{1,0:T(8,128)(2,1)}, bf16[64,2048]{1,0:T(8,128)(2,1)S(1)}, u32[]{:S(2)}) copy-start(bf16[64,2048]{1,0:T(8,128)(2,1)S(1)} %get-tuple-element.284) | copy-start | bytes 786436 | tf_op jit(solution)/shard_map/while
  21.5 1.3 copy-start
  24.1 1.8 copy-start.1
  25.6 5.2 %copy-start.3 = (bf16[64,4096]{1,0:T(8,128)(2,1)S(1)}, bf16[64,4096]{1,0:T(8,128)(2,1)}, u32[]{:S(2)}) copy-start(bf16[64,4096]{1,0:T(8,128)(2,1)} %copy-done.2) | copy-start | bytes 1572868 | tf_op jit(solution)/shard_map/while
  25.6 5.2 %copy-start.5 = (bf16[64,2048]{1,0:T(8,128)(2,1)S(1)}, bf16[64,2048]{1,0:T(8,128)(2,1)}, u32[]{:S(2)}) copy-start(bf16[64,2048]{1,0:T(8,128)(2,1)} %copy-done.4) | copy-start | bytes 786436 | tf_op jit(solution)/shard_map/while
  30.8 7.0 %copy-start.2 = (bf16[64,4096]{1,0:T(8,128)(2,1)}, bf16[64,4096]{1,0:T(8,128)(2,1)S(1)}, u32[]{:S(2)}) copy-start(bf16[64,4096]{1,0:T(8,128)(2,1)S(1)} %get-tuple-element.286) | copy-start | bytes 1572868 | tf_op jit(solution)/shard_map/while
  30.8 7.0 %copy-start.4 = (bf16[64,2048]{1,0:T(8,128)(2,1)}, bf16[64,2048]{1,0:T(8,128)(2,1)S(1)}, u32[]{:S(2)}) copy-start(bf16[64,2048]{1,0:T(8,128)(2,1)S(1)} %get-tuple-element.284) | copy-start | bytes 786436 | tf_op jit(solution)/shard_map/while
  40.1 1.3 copy-start
  42.6 2.9 %copy-start.1 = (bf16[4096,256]{0,1:T(8,128)(2,1)S(1)}, bf16[4096,256]{0,1:T(8,128)(2,1)}, u32[]{:S(2)}) copy-start(bf16[4096,256]{0,1:T(8,128)(2,1)} %copy-done) | copy-start | bytes 6291460 | tf_op jit(solution)/shard_map/while
  45.5 5.0 %copy-start.3 = (bf16[64,4096]{1,0:T(8,128)(2,1)S(1)}, bf16[64,4096]{1,0:T(8,128)(2,1)}, u32[]{:S(2)}) copy-start(bf16[64,4096]{1,0:T(8,128)(2,1)} %copy-done.2) | copy-start | bytes 1572868 | tf_op jit(solution)/shard_map/while
  45.5 5.0 %copy-start.5 = (bf16[64,2048]{1,0:T(8,128)(2,1)S(1)}, bf16[64,2048]{1,0:T(8,128)(2,1)}, u32[]{:S(2)}) copy-start(bf16[64,2048]{1,0:T(8,128)(2,1)} %copy-done.4) | copy-start | bytes 786436 | tf_op jit(solution)/shard_map/while
  50.4 7.0 %copy-start.2 = (bf16[64,4096]{1,0:T(8,128)(2,1)}, bf16[64,4096]{1,0:T(8,128)(2,1)S(1)}, u32[]{:S(2)}) copy-start(bf16[64,4096]{1,0:T(8,128)(2,1)S(1)} %get-tuple-element.286) | copy-start | bytes 1572868 | tf_op jit(solution)/shard_map/while
  50.4 7.0 %copy-start.4 = (bf16[64,2048]{1,0:T(8,128)(2,1)}, bf16[64,2048]{1,0:T(8,128)(2,1)S(1)}, u32[]{:S(2)}) copy-start(bf16[64,2048]{1,0:T(8,128)(2,1)S(1)} %get-tuple-element.284) | copy-start | bytes 786436 | tf_op jit(solution)/shard_map/while
  59.7 1.3 copy-start
  62.3 2.9 %copy-start.1 = (bf16[4096,256]{0,1:T(8,128)(2,1)S(1)}, bf16[4096,256]{0,1:T(8,128)(2,1)}, u32[]{:S(2)}) copy-start(bf16[4096,256]{0,1:T(8,128)(2,1)} %copy-done) | copy-start | bytes 6291460 | tf_op jit(solution)/shard_map/while
  65.1 5.0 %copy-start.3 = (bf16[64,4096]{1,0:T(8,128)(2,1)S(1)}, bf16[64,4096]{1,0:T(8,128)(2,1)}, u32[]{:S(2)}) copy-start(bf16[64,4096]{1,0:T(8,128)(2,1)} %copy-done.2) | copy-start | bytes 1572868 | tf_op jit(solution)/shard_map/while
  65.1 5.0 %copy-start.5 = (bf16[64,2048]{1,0:T(8,128)(2,1)S(1)}, bf16[64,2048]{1,0:T(8,128)(2,1)}, u32[]{:S(2)}) copy-start(bf16[64,2048]{1,0:T(8,128)(2,1)} %copy-done.4) | copy-start | bytes 786436 | tf_op jit(solution)/shard_map/while
  70.1 7.0 %copy-start.2 = (bf16[64,4096]{1,0:T(8,128)(2,1)}, bf16[64,4096]{1,0:T(8,128)(2,1)S(1)}, u32[]{:S(2)}) copy-start(bf16[64,4096]{1,0:T(8,128)(2,1)S(1)} %get-tuple-element.286) | copy-start | bytes 1572868 | tf_op jit(solution)/shard_map/while
  70.1 7.0 %copy-start.4 = (bf16[64,2048]{1,0:T(8,128)(2,1)}, bf16[64,2048]{1,0:T(8,128)(2,1)S(1)}, u32[]{:S(2)}) copy-start(bf16[64,2048]{1,0:T(8,128)(2,1)S(1)} %get-tuple-element.284) | copy-start | bytes 786436 | tf_op jit(solution)/shard_map/while
  79.3 1.3 copy-start
  81.9 2.9 %copy-start.1 = (bf16[4096,256]{0,1:T(8,128)(2,1)S(1)}, bf16[4096,256]{0,1:T(8,128)(2,1)}, u32[]{:S(2)}) copy-start(bf16[4096,256]{0,1:T(8,128)(2,1)} %copy-done) | copy-start | bytes 6291460 | tf_op jit(solution)/shard_map/while
  84.8 5.0 %copy-start.3 = (bf16[64,4096]{1,0:T(8,128)(2,1)S(1)}, bf16[64,4096]{1,0:T(8,128)(2,1)}, u32[]{:S(2)}) copy-start(bf16[64,4096]{1,0:T(8,128)(2,1)} %copy-done.2) | copy-start | bytes 1572868 | tf_op jit(solution)/shard_map/while
  84.8 5.0 %copy-start.5 = (bf16[64,2048]{1,0:T(8,128)(2,1)S(1)}, bf16[64,2048]{1,0:T(8,128)(2,1)}, u32[]{:S(2)}) copy-start(bf16[64,2048]{1,0:T(8,128)(2,1)} %copy-done.4) | copy-start | bytes 786436 | tf_op jit(solution)/shard_map/while
  89.8 7.0 %copy-start.2 = (bf16[64,4096]{1,0:T(8,128)(2,1)}, bf16[64,4096]{1,0:T(8,128)(2,1)S(1)}, u32[]{:S(2)}) copy-start(bf16[64,4096]{1,0:T(8,128)(2,1)S(1)} %get-tuple-element.286) | copy-start | bytes 1572868 | tf_op jit(solution)/shard_map/while
  89.8 7.0 %copy-start.4 = (bf16[64,2048]{1,0:T(8,128)(2,1)}, bf16[64,2048]{1,0:T(8,128)(2,1)S(1)}, u32[]{:S(2)}) copy-start(bf16[64,2048]{1,0:T(8,128)(2,1)S(1)} %get-tuple-element.284) | copy-start | bytes 786436 | tf_op jit(solution)/shard_map/while
  99.0 1.3 copy-start
  101.6 2.9 %copy-start.1 = (bf16[4096,256]{0,1:T(8,128)(2,1)S(1)}, bf16[4096,256]{0,1:T(8,128)(2,1)}, u32[]{:S(2)}) copy-start(bf16[4096,256]{0,1:T(8,128)(2,1)} %copy-done) | copy-start | bytes 6291460 | tf_op jit(solution)/shard_map/while
  104.4 5.0 %copy-start.3 = (bf16[64,4096]{1,0:T(8,128)(2,1)S(1)}, bf16[64,4096]{1,0:T(8,128)(2,1)}, u32[]{:S(2)}) copy-start(bf16[64,4096]{1,0:T(8,128)(2,1)} %copy-done.2) | copy-start | bytes 1572868 | tf_op jit(solution)/shard_map/while
  104.5 5.0 %copy-start.5 = (bf16[64,2048]{1,0:T(8,128)(2,1)S(1)}, bf16[64,2048]{1,0:T(8,128)(2,1)}, u32[]{:S(2)}) copy-start(bf16[64,2048]{1,0:T(8,128)(2,1)} %copy-done.4) | copy-start | bytes 786436 | tf_op jit(solution)/shard_map/while
  109.4 7.0 %copy-start.2 = (bf16[64,4096]{1,0:T(8,128)(2,1)}, bf16[64,4096]{1,0:T(8,128)(2,1)S(1)}, u32[]{:S(2)}) copy-start(bf16[64,4096]{1,0:T(8,128)(2,1)S(1)} %get-tuple-element.286) | copy-start | bytes 1572868 | tf_op jit(solution)/shard_map/while
  109.4 7.0 %copy-start.4 = (bf16[64,2048]{1,0:T(8,128)(2,1)}, bf16[64,2048]{1,0:T(8,128)(2,1)S(1)}, u32[]{:S(2)}) copy-start(bf16[64,2048]{1,0:T(8,128)(2,1)S(1)} %get-tuple-element.284) | copy-start | bytes 786436 | tf_op jit(solution)/shard_map/while
  121.2 2.9 %copy-start.1 = (bf16[4096,256]{0,1:T(8,128)(2,1)S(1)}, bf16[4096,256]{0,1:T(8,128)(2,1)}, u32[]{:S(2)}) copy-start(bf16[4096,256]{0,1:T(8,128)(2,1)} %copy-done) | copy-start | bytes 6291460 | tf_op jit(solution)/shard_map/while
  124.1 5.0 %copy-start.3 = (bf16[64,4096]{1,0:T(8,128)(2,1)S(1)}, bf16[64,4096]{1,0:T(8,128)(2,1)}, u32[]{:S(2)}) copy-start(bf16[64,4096]{1,0:T(8,128)(2,1)} %copy-done.2) | copy-start | bytes 1572868 | tf_op jit(solution)/shard_map/while
  124.1 5.0 %copy-start.5 = (bf16[64,2048]{1,0:T(8,128)(2,1)S(1)}, bf16[64,2048]{1,0:T(8,128)(2,1)}, u32[]{:S(2)}) copy-start(bf16[64,2048]{1,0:T(8,128)(2,1)} %copy-done.4) | copy-start | bytes 786436 | tf_op jit(solution)/shard_map/while
  129.1 7.0 %copy-start.2 = (bf16[64,4096]{1,0:T(8,128)(2,1)}, bf16[64,4096]{1,0:T(8,128)(2,1)S(1)}, u32[]{:S(2)}) copy-start(bf16[64,4096]{1,0:T(8,128)(2,1)S(1)} %get-tuple-element.286) | copy-start | bytes 1572868 | tf_op jit(solution)/shard_map/while
  129.1 7.0 %copy-start.4 = (bf16[64,2048]{1,0:T(8,128)(2,1)}, bf16[64,2048]{1,0:T(8,128)(2,1)S(1)}, u32[]{:S(2)}) copy-start(bf16[64,2048]{1,0:T(8,128)(2,1)S(1)} %get-tuple-element.284) | copy-start | bytes 786436 | tf_op jit(solution)/shard_map/while
  140.9 2.9 %copy-start.1 = (bf16[4096,256]{0,1:T(8,128)(2,1)S(1)}, bf16[4096,256]{0,1:T(8,128)(2,1)}, u32[]{:S(2)}) copy-start(bf16[4096,256]{0,1:T(8,128)(2,1)} %copy-done) | copy-start | bytes 6291460 | tf_op jit(solution)/shard_map/while
  143.7 5.0 %copy-start.3 = (bf16[64,4096]{1,0:T(8,128)(2,1)S(1)}, bf16[64,4096]{1,0:T(8,128)(2,1)}, u32[]{:S(2)}) copy-start(bf16[64,4096]{1,0:T(8,128)(2,1)} %copy-done.2) | copy-start | bytes 1572868 | tf_op jit(solution)/shard_map/while
  143.7 5.0 %copy-start.5 = (bf16[64,2048]{1,0:T(8,128)(2,1)S(1)}, bf16[64,2048]{1,0:T(8,128)(2,1)}, u32[]{:S(2)}) copy-start(bf16[64,2048]{1,0:T(8,128)(2,1)} %copy-done.4) | copy-start | bytes 786436 | tf_op jit(solution)/shard_map/while
  148.7 7.0 %copy-start.2 = (bf16[64,4096]{1,0:T(8,128)(2,1)}, bf16[64,4096]{1,0:T(8,128)(2,1)S(1)}, u32[]{:S(2)}) copy-start(bf16[64,4096]{1,0:T(8,128)(2,1)S(1)} %get-tuple-element.286) | copy-start | bytes 1572868 | tf_op jit(solution)/shard_map/while
  148.7 7.0 %copy-start.4 = (bf16[64,2048]{1,0:T(8,128)(2,1)}, bf16[64,2048]{1,0:T(8,128)(2,1)S(1)}, u32[]{:S(2)}) copy-start(bf16[64,2048]{1,0:T(8,128)(2,1)S(1)} %get-tuple-element.284) | copy-start | bytes 786436 | tf_op jit(solution)/shard_map/while
  160.5 2.9 %copy-start.1 = (bf16[4096,256]{0,1:T(8,128)(2,1)S(1)}, bf16[4096,256]{0,1:T(8,128)(2,1)}, u32[]{:S(2)}) copy-start(bf16[4096,256]{0,1:T(8,128)(2,1)} %copy-done) | copy-start | bytes 6291460 | tf_op jit(solution)/shard_map/while
  163.4 5.0 %copy-start.3 = (bf16[64,4096]{1,0:T(8,128)(2,1)S(1)}, bf16[64,4096]{1,0:T(8,128)(2,1)}, u32[]{:S(2)}) copy-start(bf16[64,4096]{1,0:T(8,128)(2,1)} %copy-done.2) | copy-start | bytes 1572868 | tf_op jit(solution)/shard_map/while
  163.4 5.0 %copy-start.5 = (bf16[64,2048]{1,0:T(8,128)(2,1)S(1)}, bf16[64,2048]{1,0:T(8,128)(2,1)}, u32[]{:S(2)}) copy-start(bf16[64,2048]{1,0:T(8,128)(2,1)} %copy-done.4) | copy-start | bytes 786436 | tf_op jit(solution)/shard_map/while
  168.4 58.4 %all-reduce.3.cloned.1.call-start = ((), (), s32[]{:S(2)}) async-start(), calls=%async_computation.3 | async-start | bytes 2097152 | tf_op jit(solution)/shard_map/psum | solution.py:78
  168.9 60.1 %all-gather.2.cloned.1.call-start = ((), (), s32[]{:S(2)}) async-start(), calls=%async_computation.2 | async-start | bytes 1310720 | tf_op jit(solution)/shard_map/all_gather | solution.py:83
  (3 other events, 4.0 us)
Sparse Core Ops, SparseCore 0:
  168.5 27.6 reduce-scatter.1
  199.2 16.7 all-gather.1
Sparse Core Ops, SparseCore 1:
  172.0 54.7 all-reduce.2
where the time goes:
time: 240 us; the launch traced here: 239 us
  matrix products  88.5 us (37%)
  local copies, waits for them, and re-layouts  70.8 us (30%)
  waiting for transfers between devices  55.4 us (23%)
  between operations  15.5 us (6%)
  other arithmetic  7.69 us (3%)
    while x120, local copies, waits for them, and re-layouts  42 us
    dot_general x16, matrix products, over_columns(): lax.dot_general(left, right, (((1,), (1,)), ((), ())), preferred_element_...  31.3 us
    psum x1, waiting for transfers between devices, on_device(): totals_a, totals_b = lax.psum((totals_a, totals_b), 'ind')  27.7 us
    reduce_scatter x1, waiting for transfers between devices, on_device(): share = lax.psum_scatter(stat_total, 'snp', scatter_dimension=1, tiled=True)  27.2 us
    dot_general x8, matrix products, block_terms(): allele_a = jnp.dot(q_half, ratio_a, preferred_element_type=jnp.float32)  20 us
    dot_general x8, matrix products, block_terms(): allele_b = jnp.dot(q_half, ratio_b, preferred_element_type=jnp.float32)  19.6 us
    dot_general x8, matrix products, over_rows(): lax.dot_general(left, right, (((0,), (0,)), ((), ())), preferred_element_...  17.6 us
    dynamic_slice x16, local copies, waits for them, and re-layouts, terms(): words = lax.dynamic_slice_in_dim(genotypes, start, SNP_BLOCK, 1)  15.3 us
  transfers between devices with their start and end apart: 3, of which 2 were waited for; matrix products, arithmetic and copies ran while one was open for 2% of the time, Pallas kernels for 0%

commit v1 on v0

v1 whole, which is shorter than its diff:
```python
import functools

import jax
import jax.numpy as jnp
from jax import lax
from jax.experimental import pallas as pl
from jax.experimental.pallas import tpu as pltpu
from jax.sharding import PartitionSpec as P

F32 = jnp.float32
BF16 = jnp.bfloat16
SNP_BLOCK = 512
WORD_BLOCK = 256
MESH = pl.DeviceIdType.MESH


def product(left, right, left_dim, right_dim):
    return lax.dot_general(
        left, right, (((left_dim,), (right_dim,)), ((), ())), preferred_element_type=F32
    )


def remote(src, dst, sems, recv, index, target):
    return pltpu.make_async_remote_copy(
        src_ref=src,
        dst_ref=dst,
        send_sem=sems.at[index],
        recv_sem=recv.at[index],
        device_id=target,
        device_id_type=MESH,
    )


def kernel(
    n_ind, n_snp, chunks,
    words_ref, anc_ref, freq_ref, anc_out, freq_out,
    words, q_half, q_turned, f_half, rest_half, allele, allele_in, fresh,
    stat, stat_one, stat_two, updated,
    word_sem, allele_send, allele_recv, fresh_send, fresh_recv, fresh_own,
    one_send, one_recv, two_send, two_recv, new_send, new_recv, pass_send, pass_recv, own_sem,
):
    k, people = anc_ref.shape
    columns = freq_ref.shape[1]
    height = words_ref.shape[0]
    blocks = columns // SNP_BLOCK
    tiles = height // WORD_BLOCK
    rows = k // n_ind
    half = n_snp // 2
    span = people // (chunks * n_snp)
    pieces = WORD_BLOCK // span
    per_chunk = tiles // chunks

    me = lax.axis_index("ind")
    here = lax.axis_index("snp")
    core = lax.rem(here, 2)
    place = here // 2
    mate = {"snp": here + 1 - 2 * core}

    def ind_peer(step):
        return lax.rem(me + step, n_ind)

    def place_peer(step):
        return lax.rem(place + step, half)

    def place_id(step):
        return {"snp": place_peer(step) * 2 + core}

    def word_copy(block, tile):
        start = block * SNP_BLOCK
        if not isinstance(start, int):
            start = pl.multiple_of(start, SNP_BLOCK)
        return pltpu.make_async_copy(
            words_ref.at[pl.ds(tile * WORD_BLOCK, WORD_BLOCK), pl.ds(start, SNP_BLOCK)],
            words.at[block, pl.ds(tile * WORD_BLOCK, WORD_BLOCK)],
            word_sem.at[block, tile],
        )

    for block in range(blocks):
        for tile in range(tiles):
            word_copy(block, tile).start()

    barrier = pltpu.get_barrier_semaphore()
    for step in range(1, n_ind):
        pl.semaphore_signal(barrier, 1, device_id={"ind": ind_peer(step)}, device_id_type=MESH)
    for step in range(1, half):
        pl.semaphore_signal(barrier, 1, device_id=place_id(step), device_id_type=MESH)
    pl.semaphore_signal(barrier, 1, device_id=mate, device_id_type=MESH)

    for block in range(blocks):
        cols = pl.ds(block * SNP_BLOCK, SNP_BLOCK)
        f_part = freq_ref[:, cols]
        f_half[block] = f_part.astype(BF16)
        rest_half[block] = (1.0 - f_part).astype(BF16)
    for run in range(people // WORD_BLOCK):
        cols = pl.ds(run * WORD_BLOCK, WORD_BLOCK)
        part = anc_ref[:, cols].astype(BF16)
        q_half[:, cols] = part
        q_turned[cols, :] = part.T
    stat[...] = jnp.zeros_like(stat)

    def tile_terms(block, tile):
        word_copy(block, tile).wait()
        f_part = f_half[block]
        rest_part = rest_half[block]
        packed = words[block, pl.ds(tile * WORD_BLOCK, WORD_BLOCK), :].astype(jnp.int16)
        for t in range(4):
            start = t * height + tile * WORD_BLOCK
            mixed = product(q_turned[pl.ds(start, WORD_BLOCK), :], f_part, 1, 0)
            inv_a = pltpu.reciprocal(mixed, approx=True).astype(BF16)
            inv_b = pltpu.reciprocal(1.0 - mixed, approx=True).astype(BF16)
            code = packed & jnp.int16(3 << (2 * t))
            one = code == jnp.int16(1 << (2 * t))
            two = code == jnp.int16(2 << (2 * t))
            none = code == jnp.int16(0)
            zero = jnp.zeros_like(inv_a)
            ratio_a = jnp.where(one, inv_a, jnp.where(two, inv_a + inv_a, zero))
            ratio_b = jnp.where(one, inv_b, jnp.where(none, inv_b + inv_b, zero))
            term = product(f_part, ratio_a, 1, 1) + product(rest_part, ratio_b, 1, 1)
            for piece in range(pieces):
                owner = ((tile % per_chunk) * 4 + t) * pieces + piece
                stat[tile // per_chunk, owner % 2, owner // 2] += term[:, piece * span:(piece + 1) * span]
            q_part = q_half[:, pl.ds(start, WORD_BLOCK)]
            sum_a = product(q_part, ratio_a, 1, 0)
            sum_b = product(q_part, ratio_b, 1, 0)
            if tile == 0 and t == 0:
                allele[block, 0] = sum_a
                allele[block, 1] = sum_b
            else:
                allele[block, 0] += sum_a
                allele[block, 1] += sum_b

    def own_rows(owner):
        return pl.ds(pl.multiple_of(owner * rows, rows), rows)

    def allele_copy(block, step):
        peer = ind_peer(step)
        return remote(
            allele.at[block, :, own_rows(peer)], allele_in.at[block, step - 1],
            allele_send, allele_recv, (block, step - 1), {"ind": peer},
        )

    def fresh_place(block):
        start = block * SNP_BLOCK
        if not isinstance(start, int):
            start = pl.multiple_of(start, SNP_BLOCK)
        return freq_out.at[own_rows(me), pl.ds(start, SNP_BLOCK)]

    def fresh_copy(block, step):
        return remote(
            fresh.at[block], fresh_place(block),
            fresh_send, fresh_recv, (block, step - 1), {"ind": ind_peer(step)},
        )

    def fresh_keep(block):
        return pltpu.make_async_copy(fresh.at[block], fresh_place(block), fresh_own.at[block])

    def allele_start(block):
        for step in range(1, n_ind):
            allele_copy(block, step).start()

    def allele_finish(block):
        total = allele[block, :, own_rows(me), :]
        for step in range(1, n_ind):
            allele_copy(block, step).wait_recv()
            total = total + allele_in[block, step - 1]
        start = block * SNP_BLOCK
        if not isinstance(start, int):
            start = pl.multiple_of(start, SNP_BLOCK)
        current = freq_ref[own_rows(me), pl.ds(start, SNP_BLOCK)]
        upper = current * total[0]
        fresh[block] = upper / (upper + (1.0 - current) * total[1])
        for step in range(1, n_ind):
            fresh_copy(block, step).start()
        fresh_keep(block).start()

    def one_copy(chunk):
        return remote(
            stat.at[chunk, 1 - core], stat_one.at[chunk], one_send, one_recv, chunk, mate
        )

    def two_copy(chunk, step):
        return remote(
            stat.at[chunk, core, place_peer(step)], stat_two.at[chunk, step - 1],
            two_send, two_recv, (chunk, step - 1), place_id(step),
        )

    def individuals(chunk, owner):
        run = owner // pieces
        tile = chunk * per_chunk + run // 4
        start = lax.rem(run, 4) * height + tile * WORD_BLOCK + lax.rem(owner, pieces) * span
        return pl.ds(pl.multiple_of(start, span), span)

    def new_copy(chunk, step):
        return remote(
            updated.at[chunk], anc_out.at[:, individuals(chunk, here)],
            new_send, new_recv, (chunk, step - 1), place_id(step),
        )

    def new_mate(chunk):
        return remote(
            updated.at[chunk], anc_out.at[:, individuals(chunk, here)],
            new_send, new_recv, (chunk, half - 1), mate,
        )

    def new_keep(chunk):
        return pltpu.make_async_copy(
            updated.at[chunk], anc_out.at[:, individuals(chunk, here)], own_sem.at[chunk]
        )

    def pass_copy(chunk, step):
        owner = lax.rem(place + half - step, half) * 2 + core
        part = anc_out.at[:, individuals(chunk, owner)]
        return remote(part, part, pass_send, pass_recv, (chunk, step - 1), mate)

    def stat_send(chunk):
        one_copy(chunk).start()

    def stat_pair(chunk):
        one_copy(chunk).wait()
        for step in range(1, half):
            peer = place_peer(step)
            stat[chunk, core, peer] += stat_one[chunk, peer]
            two_copy(chunk, step).start()
        stat[chunk, core, place] += stat_one[chunk, place]

    def stat_new(chunk):
        total = stat[chunk, core, place]
        for step in range(1, half):
            two_copy(chunk, step).wait_recv()
            total = total + stat_two[chunk, step - 1]
        weighted = anc_ref[:, individuals(chunk, here)] * total
        updated[chunk] = k * weighted / jnp.sum(weighted, axis=0, keepdims=True)
        for step in range(1, half):
            new_copy(chunk, step).start()
        new_mate(chunk).start()
        new_keep(chunk).start()

    def stat_pass(chunk):
        for step in range(1, half):
            new_copy(chunk, step).wait_recv()
            pass_copy(chunk, step).start()

    stages = (stat_send, stat_pair, stat_new, stat_pass)

    def tick(now):
        for stage, act in enumerate(stages):
            if 0 <= now - stage < chunks:
                act(now - stage)

    def sweep(block, carry):
        for tile in range(tiles):
            tile_terms(block, tile)

        @pl.when(block == 0)
        def _():
            pl.semaphore_wait(barrier, n_ind - 1 + half)

        allele_start(block)

        @pl.when(block > 0)
        def _():
            allele_finish(block - 1)

        return carry

    last = blocks - 1
    lax.fori_loop(0, last, sweep, 0)
    for tile in range(tiles):
        tile_terms(last, tile)
        if tile == tiles - 1:
            allele_start(last)
        if (tile + 1) % per_chunk == 0:
            tick(tile // per_chunk)
    allele_finish(last - 1)
    tick(chunks)
    tick(chunks + 1)
    allele_finish(last)
    tick(chunks + 2)

    for chunk in range(chunks):
        for step in range(1, half):
            two_copy(chunk, step).wait_send()
            new_copy(chunk, step).wait_send()
            pass_copy(chunk, step).wait()
        new_mate(chunk).wait()
        new_keep(chunk).wait()
    for block in range(blocks):
        for step in range(1, n_ind):
            allele_copy(block, step).wait_send()
            fresh_copy(block, step).wait()
        fresh_keep(block).wait()


def on_device(n_ind, n_snp, genotypes, ancestry, frequency):
    k, people = ancestry.shape
    columns = frequency.shape[1]
    height = genotypes.shape[0]
    blocks = columns // SNP_BLOCK
    tiles = height // WORD_BLOCK
    half = n_snp // 2
    chunks = min(tiles, people // (n_snp * 128))
    span = people // (chunks * n_snp)
    rows = k // n_ind
    dma = pltpu.SemaphoreType.DMA
    vmem = pl.BlockSpec(memory_space=pltpu.VMEM)
    anywhere = pl.BlockSpec(memory_space=pl.ANY)
    return pl.pallas_call(
        functools.partial(kernel, n_ind, n_snp, chunks),
        out_shape=(
            jax.ShapeDtypeStruct(ancestry.shape, F32),
            jax.ShapeDtypeStruct(frequency.shape, F32),
        ),
        in_specs=[anywhere, vmem, vmem],
        out_specs=(anywhere, anywhere),
        scratch_shapes=[
            pltpu.VMEM((blocks, height, SNP_BLOCK), jnp.int32),
            pltpu.VMEM((k, people), BF16),
            pltpu.VMEM((people, k), BF16),
            pltpu.VMEM((blocks, k, SNP_BLOCK), BF16),
            pltpu.VMEM((blocks, k, SNP_BLOCK), BF16),
            pltpu.VMEM((blocks, 2, k, SNP_BLOCK), F32),
            pltpu.VMEM((blocks, n_ind - 1, 2, rows, SNP_BLOCK), F32),
            pltpu.VMEM((blocks, rows, SNP_BLOCK), F32),
            pltpu.VMEM((chunks, 2, half, k, span), F32),
            pltpu.VMEM((chunks, half, k, span), F32),
            pltpu.VMEM((chunks, half - 1, k, span), F32),
            pltpu.VMEM((chunks, k, span), F32),
            dma((blocks, tiles)),
            dma((blocks, n_ind - 1)),
            dma((blocks, n_ind - 1)),
            dma((blocks, n_ind - 1)),
            dma((blocks, n_ind - 1)),
            dma((blocks,)),
            dma((chunks,)),
            dma((chunks,)),
            dma((chunks, half - 1)),
            dma((chunks, half - 1)),
            dma((chunks, half)),
            dma((chunks, half)),
            dma((chunks, half - 1)),
            dma((chunks, half - 1)),
            dma((chunks,)),
        ],
        compiler_params=pltpu.CompilerParams(
            collective_id=0, has_side_effects=True, vmem_limit_bytes=48 * 2**20
        ),
        name="admixture_step",
    )(genotypes, ancestry, frequency)


def solution(mesh):
    placed = (P(("group", "ind"), "snp"), P(None, ("group", "ind")), P(None, ("group", "snp")))
    return jax.shard_map(
        functools.partial(on_device, mesh.shape["ind"], mesh.shape["snp"]),
        mesh=mesh,
        in_specs=placed,
        out_specs=(P(None, ("group", "ind")), P(None, ("group", "snp"))),
        check_vma=False,
    )
```

time: 240 us -> 54.7 us (0.23)
  matrix products: 88.5 us -> 0 us
  local copies, waits for them, and re-layouts: 70.8 us -> 4.02 us
  waiting for transfers between devices: 55.4 us -> 0 us
  Pallas kernels: 0 us -> 49.9 us
  between operations: 15.5 us -> 0.65 us
  other arithmetic: 7.69 us -> 0 us
    dot_general x40 -> x0, matrix products: 88.5 us -> none  [the longest x16 31.3 us: over_columns(): lax.dot_general(left, right, (((1,), (1,)), ((), ())), preferred_element_...]
    pallas_call x0 -> x1, Pallas kernels: none -> 49.9 us  [on_device(): pl.pallas_call(functools.partial(kernel, n_ind, n_snp, chunks), out_shape...]
    while x120 -> x0, local copies, waits for them, and re-layouts: 42 us -> none
    psum x1 -> x0, waiting for transfers between devices: 27.7 us -> none  [on_device(): totals_a, totals_b = lax.psum((totals_a, totals_b), 'ind')]
    reduce_scatter x1 -> x0, waiting for transfers between devices: 27.2 us -> none  [on_device(): share = lax.psum_scatter(stat_total, 'snp', scatter_dimension=1, tiled=True)]
    dynamic_slice x16 -> x0, local copies, waits for them, and re-layouts: 15.3 us -> none  [terms(): words = lax.dynamic_slice_in_dim(genotypes, start, SNP_BLOCK, 1)]
    shift_right_arithmetic x8 -> x0, local copies, waits for them, and re-layouts: 9.56 us -> none  [unpack(): codes = words[None] >> shifts[:, None, None] & 3]
    div x2 -> x0, other arithmetic: 4.04 us -> none  [the longest x1 2.26 us: refresh(): return upper_part / (upper_part + (1.0 - current) * allele_b)]
  transfers between devices with their start and end apart: 3 -> 0, of which waited for: 2 -> 0; matrix products, arithmetic and copies ran while one was open for 2% -> 0% of each run, Pallas kernels for 0% -> 0%
where the time goes in v1:
time: 54.7 us; the launch traced here: 54.5 us
  Pallas kernels  49.9 us (91%)
  local copies, waits for them, and re-layouts  4.02 us (7%)
  between operations  0.65 us (1%)
    pallas_call x1, Pallas kernels, on_device(): pl.pallas_call(functools.partial(kernel, n_ind, n_snp, chunks), out_shape...  49.9 us
    unnamed x6, local copies, waits for them, and re-layouts  4.02 us

profile of v1, /device:TPU:0, one launch (start us, length us, event | category | flops | bytes accessed | tf_op | source)
XLA Modules:
  0.0 54.5 jit_solution(517010009440940361)
XLA Ops:
  0.6 0.0 copy-start
  0.6 1.2 %copy-done = f32[64,4096]{1,0:T(8,128)S(1)} copy-done((f32[64,4096]{1,0:T(8,128)S(1)}, f32[64,4096]{1,0:T(8,128)}, u32[]{:S(2)}) %copy-start) | copy-done | bytes 1048600
  1.9 0.0 copy-start.1
  1.9 1.0 %copy-done.1 = f32[64,2048]{1,0:T(8,128)S(1)} copy-done((f32[64,2048]{1,0:T(8,128)S(1)}, f32[64,2048]{1,0:T(8,128)}, u32[]{:S(2)}) %copy-start.1) | copy-done | bytes 524312
  2.9 49.9 %admixture_step.1 = (f32[64,4096]{1,0:T(8,128)S(1)}, f32[64,2048]{1,0:T(8,128)S(1)}) custom-call(s32[1024,2048]{1,0:T(8,128)} %words_ref.1, f32[64,4096]{1,0:T(8,128)S(1)} %copy-done, f32[64,2048]{1,0:T(8,128)S(1)} %copy-done.1), custom_call_target="tpu_custom_call" | custom-call | tf_op jit(solution)/shard_map/admixture_step/pallas_call | solution.py:307
  52.8 1.0 %copy.7 = f32[64,4096]{1,0:T(8,128)} copy(f32[64,4096]{1,0:T(8,128)S(1)} %get-tuple-element.4) | data formatting | bytes 2097152
  53.7 0.8 %copy.8 = f32[64,2048]{1,0:T(8,128)} copy(f32[64,2048]{1,0:T(8,128)S(1)} %get-tuple-element.5) | data formatting | bytes 1048576
Async XLA Ops:
  0.6 1.2 %copy-start = (f32[64,4096]{1,0:T(8,128)S(1)}, f32[64,4096]{1,0:T(8,128)}, u32[]{:S(2)}) copy-start(f32[64,4096]{1,0:T(8,128)} %anc_ref.1) | copy-start | bytes 3145732
  1.9 1.0 %copy-start.1 = (f32[64,2048]{1,0:T(8,128)S(1)}, f32[64,2048]{1,0:T(8,128)}, u32[]{:S(2)}) copy-start(f32[64,2048]{1,0:T(8,128)} %freq_ref.1) | copy-start | bytes 1572868

commit v2 on v1

--- a/solution.py
+++ b/solution.py
@@ -34,9 +34,10 @@
 def kernel(
     n_ind, n_snp, chunks,
     words_ref, anc_ref, freq_ref, anc_out, freq_out,
-    words, q_half, q_turned, f_half, rest_half, allele, allele_in, fresh,
+    words, q_half, q_turned, f_half, rest_half, allele, allele_one, allele_two, allele_in, fresh,
     stat, stat_one, stat_two, updated,
-    word_sem, allele_send, allele_recv, fresh_send, fresh_recv, fresh_own,
+    word_sem, half_send, half_recv, allele_send, allele_recv, fresh_send, fresh_recv, fresh_own,
+    hand_send, hand_recv, direct_send, direct_recv, last_send, last_recv,
     one_send, one_recv, two_send, two_recv, new_send, new_recv, pass_send, pass_recv, own_sem,
 ):
     k, people = anc_ref.shape
@@ -44,13 +45,19 @@
     height = words_ref.shape[0]
     blocks = columns // SNP_BLOCK
     tiles = height // WORD_BLOCK
+    last = blocks - 1
     rows = k // n_ind
     half = n_snp // 2
+    depth = n_ind // 2
+    side_rows = k // 2
     span = people // (chunks * n_snp)
     pieces = WORD_BLOCK // span
     per_chunk = tiles // chunks
 
     me = lax.axis_index("ind")
+    side = lax.rem(me, 2)
+    level = me // 2
+    neighbour = {"ind": me + 1 - 2 * side}
     here = lax.axis_index("snp")
     core = lax.rem(here, 2)
     place = here // 2
@@ -58,6 +65,12 @@
 
     def ind_peer(step):
         return lax.rem(me + step, n_ind)
+
+    def level_peer(step):
+        return lax.rem(level + step, depth)
+
+    def level_id(step):
+        return {"ind": level_peer(step) * 2 + side}
 
     def place_peer(step):
         return lax.rem(place + step, half)
@@ -129,49 +142,105 @@
                 allele[block, 0] += sum_a
                 allele[block, 1] += sum_b
 
-    def own_rows(owner):
-        return pl.ds(pl.multiple_of(owner * rows, rows), rows)
+    def own_rows(spot):
+        return pl.ds(pl.multiple_of(side * side_rows + spot * rows, rows), rows)
+
+    def half_copy(block):
+        other = pl.ds(pl.multiple_of((1 - side) * side_rows, side_rows), side_rows)
+        return remote(
+            allele.at[block, :, other], allele_one.at[block], half_send, half_recv, block, neighbour
+        )
 
     def allele_copy(block, step):
-        peer = ind_peer(step)
-        return remote(
-            allele.at[block, :, own_rows(peer)], allele_in.at[block, step - 1],
-            allele_send, allele_recv, (block, step - 1), {"ind": peer},
-        )
-
-    def fresh_place(block):
+        return remote(
+            allele.at[block, :, own_rows(level_peer(step))], allele_two.at[block, step - 1],
+            allele_send, allele_recv, (block, step - 1), level_id(step),
+        )
+
+    def block_columns(block):
         start = block * SNP_BLOCK
         if not isinstance(start, int):
             start = pl.multiple_of(start, SNP_BLOCK)
-        return freq_out.at[own_rows(me), pl.ds(start, SNP_BLOCK)]
+        return pl.ds(start, SNP_BLOCK)
+
+    def fresh_place(block, spot):
+        return freq_out.at[own_rows(spot), block_columns(block)]
 
     def fresh_copy(block, step):
         return remote(
-            fresh.at[block], fresh_place(block),
-            fresh_send, fresh_recv, (block, step - 1), {"ind": ind_peer(step)},
+            fresh.at[block], fresh_place(block, level),
+            fresh_send, fresh_recv, (block, step - 1), level_id(step),
+        )
+
+    def fresh_near(block):
+        return remote(
+            fresh.at[block], fresh_place(block, level),
+            fresh_send, fresh_recv, (block, depth - 1), neighbour,
         )
 
     def fresh_keep(block):
-        return pltpu.make_async_copy(fresh.at[block], fresh_place(block), fresh_own.at[block])
+        return pltpu.make_async_copy(fresh.at[block], fresh_place(block, level), fresh_own.at[block])
+
+    def hand_copy(block, step):
+        part = fresh_place(block, lax.rem(level + depth - step, depth))
+        return remote(part, part, hand_send, hand_recv, (block, step - 1), neighbour)
 
     def allele_start(block):
-        for step in range(1, n_ind):
+        half_copy(block).start()
+
+    def allele_pair(block):
+        half_copy(block).wait()
+        for step in range(1, depth):
+            spot = level_peer(step)
+            near = pl.ds(pl.multiple_of(spot * rows, rows), rows)
+            allele[block, :, own_rows(spot), :] += allele_one[block, :, near, :]
             allele_copy(block, step).start()
+        near = pl.ds(pl.multiple_of(level * rows, rows), rows)
+        allele[block, :, own_rows(level), :] += allele_one[block, :, near, :]
 
     def allele_finish(block):
-        total = allele[block, :, own_rows(me), :]
-        for step in range(1, n_ind):
+        total = allele[block, :, own_rows(level), :]
+        for step in range(1, depth):
             allele_copy(block, step).wait_recv()
-            total = total + allele_in[block, step - 1]
-        start = block * SNP_BLOCK
-        if not isinstance(start, int):
-            start = pl.multiple_of(start, SNP_BLOCK)
-        current = freq_ref[own_rows(me), pl.ds(start, SNP_BLOCK)]
+            total = total + allele_two[block, step - 1]
+        current = freq_ref[own_rows(level), block_columns(block)]
         upper = current * total[0]
         fresh[block] = upper / (upper + (1.0 - current) * total[1])
+        for step in range(1, depth):
+            fresh_copy(block, step).start()
+        fresh_near(block).start()
+        fresh_keep(block).start()
+
+    def allele_hand(block):
+        for step in range(1, depth):
+            fresh_copy(block, step).wait_recv()
+            hand_copy(block, step).start()
+
+    def direct_copy(step):
+        peer = ind_peer(step)
+        start = lax.rem(peer, 2) * side_rows + peer // 2 * rows
+        return remote(
+            allele.at[last, :, pl.ds(pl.multiple_of(start, rows), rows)], allele_in.at[step - 1],
+            direct_send, direct_recv, step - 1, {"ind": peer},
+        )
+
+    def last_copy(step):
+        return remote(
+            fresh.at[last], fresh_place(last, level),
+            last_send, last_recv, step - 1, {"ind": ind_peer(step)},
+        )
+
+    def direct_finish():
+        total = allele[last, :, own_rows(level), :]
         for step in range(1, n_ind):
-            fresh_copy(block, step).start()
-        fresh_keep(block).start()
+            direct_copy(step).wait_recv()
+            total = total + allele_in[step - 1]
+        current = freq_ref[own_rows(level), block_columns(last)]
+        upper = current * total[0]
+        fresh[last] = upper / (upper + (1.0 - current) * total[1])
+        for step in range(1, n_ind):
+            last_copy(step).start()
+        fresh_keep(last).start()
 
     def one_copy(chunk):
         return remote(
@@ -259,23 +328,39 @@
 
         @pl.when(block > 0)
         def _():
-            allele_finish(block - 1)
+            allele_pair(block - 1)
+
+        @pl.when(block > 1)
+        def _():
+            allele_finish(block - 2)
 
         return carry
 
-    last = blocks - 1
     lax.fori_loop(0, last, sweep, 0)
     for tile in range(tiles):
         tile_terms(last, tile)
+        if tile == tiles - 2:
+            allele_pair(last - 1)
+            allele_finish(last - 2)
+            for block in range(last - 2):
+                allele_hand(block)
         if tile == tiles - 1:
-            allele_start(last)
+            for step in range(1, n_ind):
+                direct_copy(step).start()
         if (tile + 1) % per_chunk == 0:
             tick(tile // per_chunk)
+    end = chunks - 1
+    stat_pair(end)
+    if end > 1:
+        stat_pass(end - 2)
+    stat_new(end - 1)
     allele_finish(last - 1)
-    tick(chunks)
-    tick(chunks + 1)
-    allele_finish(last)
-    tick(chunks + 2)
+    allele_hand(last - 2)
+    stat_new(end)
+    stat_pass(end - 1)
+    direct_finish()
+    allele_hand(last - 1)
+    stat_pass(end)
 
     for chunk in range(chunks):
         for step in range(1, half):
@@ -284,11 +369,17 @@
             pass_copy(chunk, step).wait()
         new_mate(chunk).wait()
         new_keep(chunk).wait()
-    for block in range(blocks):
-        for step in range(1, n_ind):
+    for block in range(last):
+        for step in range(1, depth):
             allele_copy(block, step).wait_send()
-            fresh_copy(block, step).wait()
+            fresh_copy(block, step).wait_send()
+            hand_copy(block, step).wait()
+        fresh_near(block).wait()
         fresh_keep(block).wait()
+    for step in range(1, n_ind):
+        direct_copy(step).wait_send()
+        last_copy(step).wait()
+    fresh_keep(last).wait()
 
 
 def on_device(n_ind, n_snp, genotypes, ancestry, frequency):
@@ -298,6 +389,7 @@
     blocks = columns // SNP_BLOCK
     tiles = height // WORD_BLOCK
     half = n_snp // 2
+    depth = n_ind // 2
     chunks = min(tiles, people // (n_snp * 128))
     span = people // (chunks * n_snp)
     rows = k // n_ind
@@ -319,18 +411,28 @@
             pltpu.VMEM((blocks, k, SNP_BLOCK), BF16),
             pltpu.VMEM((blocks, k, SNP_BLOCK), BF16),
             pltpu.VMEM((blocks, 2, k, SNP_BLOCK), F32),
-            pltpu.VMEM((blocks, n_ind - 1, 2, rows, SNP_BLOCK), F32),
+            pltpu.VMEM((blocks, 2, k // 2, SNP_BLOCK), F32),
+            pltpu.VMEM((blocks, depth - 1, 2, rows, SNP_BLOCK), F32),
+            pltpu.VMEM((n_ind - 1, 2, rows, SNP_BLOCK), F32),
             pltpu.VMEM((blocks, rows, SNP_BLOCK), F32),
             pltpu.VMEM((chunks, 2, half, k, span), F32),
             pltpu.VMEM((chunks, half, k, span), F32),
             pltpu.VMEM((chunks, half - 1, k, span), F32),
             pltpu.VMEM((chunks, k, span), F32),
             dma((blocks, tiles)),
-            dma((blocks, n_ind - 1)),
-            dma((blocks, n_ind - 1)),
-            dma((blocks, n_ind - 1)),
-            dma((blocks, n_ind - 1)),
             dma((blocks,)),
+            dma((blocks,)),
+            dma((blocks, depth - 1)),
+            dma((blocks, depth - 1)),
+            dma((blocks, depth)),
+            dma((blocks, depth)),
+            dma((blocks,)),
+            dma((blocks, depth - 1)),
+            dma((blocks, depth - 1)),
+            dma((n_ind - 1,)),
+            dma((n_ind - 1,)),
+            dma((n_ind - 1,)),
+            dma((n_ind - 1,)),
             dma((chunks,)),
             dma((chunks,)),
             dma((chunks, half - 1)),

time: 54.7 us -> 52.8 us (0.965)
  Pallas kernels: 49.9 us -> 47.9 us
    pallas_call x1, Pallas kernels: 49.9 us -> 47.9 us  [on_device(): pl.pallas_call(functools.partial(kernel, n_ind, n_snp, chunks), out_shape...]
where the time goes in v2:
time: 52.8 us; the launch traced here: 52.6 us
  Pallas kernels  47.9 us (91%)
  local copies, waits for them, and re-layouts  4.02 us (8%)
  between operations  0.65 us (1%)
    pallas_call x1, Pallas kernels, on_device(): pl.pallas_call(functools.partial(kernel, n_ind, n_snp, chunks), out_shape...  47.9 us
    unnamed x6, local copies, waits for them, and re-layouts  4.02 us

profile of v2, /device:TPU:0, one launch (start us, length us, event | category | flops | bytes accessed | tf_op | source)
XLA Modules:
  0.0 52.6 jit_solution(2542088874994703931)
XLA Ops:
  0.6 0.0 copy-start
  0.6 1.2 %copy-done = f32[64,4096]{1,0:T(8,128)S(1)} copy-done((f32[64,4096]{1,0:T(8,128)S(1)}, f32[64,4096]{1,0:T(8,128)}, u32[]{:S(2)}) %copy-start) | copy-done | bytes 1048600
  1.9 0.0 copy-start.1
  1.9 1.0 %copy-done.1 = f32[64,2048]{1,0:T(8,128)S(1)} copy-done((f32[64,2048]{1,0:T(8,128)S(1)}, f32[64,2048]{1,0:T(8,128)}, u32[]{:S(2)}) %copy-start.1) | copy-done | bytes 524312
  2.9 47.9 %admixture_step.1 = (f32[64,4096]{1,0:T(8,128)S(1)}, f32[64,2048]{1,0:T(8,128)S(1)}) custom-call(s32[1024,2048]{1,0:T(8,128)} %words_ref.1, f32[64,4096]{1,0:T(8,128)S(1)} %copy-done, f32[64,2048]{1,0:T(8,128)S(1)} %copy-done.1), custom_call_target="tpu_custom_call" | custom-call | tf_op jit(solution)/shard_map/admixture_step/pallas_call | solution.py:399
  50.8 1.0 %copy.7 = f32[64,4096]{1,0:T(8,128)} copy(f32[64,4096]{1,0:T(8,128)S(1)} %get-tuple-element.4) | data formatting | bytes 2097152
  51.8 0.8 %copy.8 = f32[64,2048]{1,0:T(8,128)} copy(f32[64,2048]{1,0:T(8,128)S(1)} %get-tuple-element.5) | data formatting | bytes 1048576
Async XLA Ops:
  0.6 1.2 %copy-start = (f32[64,4096]{1,0:T(8,128)S(1)}, f32[64,4096]{1,0:T(8,128)}, u32[]{:S(2)}) copy-start(f32[64,4096]{1,0:T(8,128)} %anc_ref.1) | copy-start | bytes 3145732
  1.9 1.0 %copy-start.1 = (f32[64,2048]{1,0:T(8,128)S(1)}, f32[64,2048]{1,0:T(8,128)}, u32[]{:S(2)}) copy-start(f32[64,2048]{1,0:T(8,128)} %freq_ref.1) | copy-start | bytes 1572868

commit v3 on v2

--- a/solution.py
+++ b/solution.py
@@ -353,12 +353,12 @@
     stat_pair(end)
     if end > 1:
         stat_pass(end - 2)
+    allele_finish(last - 1)
     stat_new(end - 1)
-    allele_finish(last - 1)
+    stat_new(end)
+    direct_finish()
     allele_hand(last - 2)
-    stat_new(end)
     stat_pass(end - 1)
-    direct_finish()
     allele_hand(last - 1)
     stat_pass(end)
 

time: 52.8 us -> 53.2 us (level)
  no operation moved by 1% of the time
where the time goes in v3:
time: 53.2 us; the launch traced here: 53 us
  Pallas kernels  48.3 us (91%)
  local copies, waits for them, and re-layouts  4.02 us (8%)
  between operations  0.65 us (1%)
    pallas_call x1, Pallas kernels, on_device(): pl.pallas_call(functools.partial(kernel, n_ind, n_snp, chunks), out_shape...  48.3 us
    unnamed x6, local copies, waits for them, and re-layouts  4.02 us

profile of v3, /device:TPU:0, one launch (start us, length us, event | category | flops | bytes accessed | tf_op | source)
XLA Modules:
  0.0 53.0 jit_solution(10080903247839384776)
XLA Ops:
  0.6 0.0 copy-start
  0.6 1.2 %copy-done = f32[64,4096]{1,0:T(8,128)S(1)} copy-done((f32[64,4096]{1,0:T(8,128)S(1)}, f32[64,4096]{1,0:T(8,128)}, u32[]{:S(2)}) %copy-start) | copy-done | bytes 1048600
  1.9 0.0 copy-start.1
  1.9 1.0 %copy-done.1 = f32[64,2048]{1,0:T(8,128)S(1)} copy-done((f32[64,2048]{1,0:T(8,128)S(1)}, f32[64,2048]{1,0:T(8,128)}, u32[]{:S(2)}) %copy-start.1) | copy-done | bytes 524312
  2.9 48.3 %admixture_step.1 = (f32[64,4096]{1,0:T(8,128)S(1)}, f32[64,2048]{1,0:T(8,128)S(1)}) custom-call(s32[1024,2048]{1,0:T(8,128)} %words_ref.1, f32[64,4096]{1,0:T(8,128)S(1)} %copy-done, f32[64,2048]{1,0:T(8,128)S(1)} %copy-done.1), custom_call_target="tpu_custom_call" | custom-call | tf_op jit(solution)/shard_map/admixture_step/pallas_call | solution.py:399
  51.2 1.0 %copy.7 = f32[64,4096]{1,0:T(8,128)} copy(f32[64,4096]{1,0:T(8,128)S(1)} %get-tuple-element.4) | data formatting | bytes 2097152
  52.2 0.8 %copy.8 = f32[64,2048]{1,0:T(8,128)} copy(f32[64,2048]{1,0:T(8,128)S(1)} %get-tuple-element.5) | data formatting | bytes 1048576
Async XLA Ops:
  0.6 1.2 %copy-start = (f32[64,4096]{1,0:T(8,128)S(1)}, f32[64,4096]{1,0:T(8,128)}, u32[]{:S(2)}) copy-start(f32[64,4096]{1,0:T(8,128)} %anc_ref.1) | copy-start | bytes 3145732
  1.9 1.0 %copy-start.1 = (f32[64,2048]{1,0:T(8,128)S(1)}, f32[64,2048]{1,0:T(8,128)}, u32[]{:S(2)}) copy-start(f32[64,2048]{1,0:T(8,128)} %freq_ref.1) | copy-start | bytes 1572868
